TPU v7x, 32 devices: a whole 2x2x4 slice. The times are simulated.
32 devices in a mesh: grp: 2 (over y), ctg: 4 (over z), line: 4 (over x, core).
Axes of the slice: x: 2, y: 2, z: 4, core: 2. Of those that a mesh axis runs over, the one named last changes fastest.
Arguments:
- owned_flow: float32 [4, 24, 5120], P('line', 'grp', 'ctg'), parts along dimension 1, may hold values from -6 to 6
- ratings: float32 [20480], P('line'), may hold values from 0.8 to 3
- lodf_tiles: bfloat16 [4, 32, 128, 128], P('ctg', 'line'), may hold values from -2.5 to 2.5
- tile_map: int32 [4, 160], P('ctg', 'line'), may hold values from -1 to 7, as said below
- outage_line: int32 [512], P('ctg'), may hold values from 0 to 20479, as said below
- block_owner: int32 [4], replicated, may hold values from 0 to 3, each once
- multipliers: float32 [4, 32, 24, 128, 128], P('ctg', 'line', 'grp'), parts along dimension 2, may hold values from 0.05 to 2
Outputs:
- new_multipliers: float32 [4, 32, 24, 128, 128], P('ctg', 'line', 'grp'), parts along dimension 2
- line_gradient: float32 [4, 24, 5120], P('line', 'grp', 'ctg'), parts along dimension 1
- outage_gradient: float32 [24, 512], P('grp', 'ctg'), parts along dimension 0
There are 2 independent parts, one for each index of `grp`. A program takes and returns all parts, laid end to end along the dimension named above; an argument that names none is the same for every part. Nothing has to cross between parts.
Inputs may be any that keep to these rules, and one draw needn't show every extreme that they name: `tile_map`: in each row and each run of B = 40 columns of a line shard, the slots 0 to n - 1 appear once each for some n of at least 2, and the other entries are -1; every line shard has n = 8 in some row. `outage_line`: no two contingencies take out the same line. `block_owner`: each owner slot names a different block.
All inputs are finite; a program needn't handle non-finite values.
Results may differ from a plain program's by a relative error of at most 0.0003.
Values sent between devices are 32-bit elements; how exact they have to be, the bound alone decides.
A program may use at most 128 MiB of HBM per device.

v0:
```python
import jax
import jax.numpy as jnp
from jax import lax
from jax.sharding import PartitionSpec as P

dual_step = 0.5
outage_scale = 0.0625


def tile_step(tiles, slot_map, flow_rows, rating_rows, outage_flow, multipliers):
    slots = tiles.shape[0]
    match = (slot_map[:, None] == jnp.arange(slots, dtype=jnp.int32)[None, :]).astype(jnp.float32)
    slot_flow = jnp.einsum("bs,hbl->shl", match, flow_rows, precision=lax.Precision.HIGHEST)
    slot_rating = jnp.einsum("bs,bl->sl", match, rating_rows, precision=lax.Precision.HIGHEST)
    present = jnp.sum(match, axis=0)
    safe_rating = slot_rating + (1.0 - present)[:, None]
    inverse = 1.0 / (safe_rating * safe_rating)
    lodf = tiles.astype(jnp.float32)
    post = slot_flow[:, :, None, :] + lodf[:, None, :, :] * outage_flow[None, :, :, None]
    raised = multipliers + dual_step * (post * post * inverse[:, None, None, :] - 1.0)
    updated = jnp.maximum(raised, 0.0) * present[:, None, None, None]
    weight = updated * post * inverse[:, None, None, :]
    direct = jnp.sum(weight, axis=2)
    line_part = jnp.einsum("bs,shl->hbl", match, direct, precision=lax.Precision.HIGHEST)
    outage_part = jnp.sum(lodf[:, None, :, :] * weight, axis=(0, 3))
    return (updated, line_part, outage_part)


def per_device(owned_flow, ratings, lodf_tiles, tile_map, outage_line, block_owner, multipliers):
    hours = owned_flow.shape[1]
    piece = owned_flow.shape[2]
    ctg_count = lax.axis_size("ctg")
    line_count = lax.axis_size("line")
    shard_lines = ratings.shape[0]
    tile = lodf_tiles.shape[-1]
    kblocks = lodf_tiles.shape[0]
    outages = outage_line.shape[0] * ctg_count
    inverse_owner = (
        jnp.zeros_like(block_owner).at[block_owner].set(jnp.arange(ctg_count, dtype=jnp.int32))
    )
    gathered = lax.all_gather(owned_flow, ("ctg", "line"), axis=0, tiled=True)
    shaped = jnp.take(gathered.reshape(ctg_count, line_count, hours, piece), inverse_owner, axis=0)
    every_flow = shaped.transpose(2, 1, 0, 3).reshape(hours, line_count * shard_lines)
    shard_flow = lax.dynamic_slice_in_dim(
        every_flow, lax.axis_index("line") * shard_lines, shard_lines, 1
    )
    outage_flow = jnp.take(every_flow, outage_line, axis=1)
    flow_rows = shard_flow.reshape(hours, shard_lines // tile, tile)
    rating_rows = ratings.reshape(shard_lines // tile, tile)
    outage_blocks = outage_flow.reshape(hours, kblocks, tile).transpose(1, 0, 2)
    updated, line_part, outage_part = jax.vmap(tile_step, in_axes=(0, 0, None, None, 0, 0))(
        lodf_tiles, tile_map, flow_rows, rating_rows, outage_blocks, multipliers
    )
    line_sum = jnp.sum(line_part, axis=0).reshape(hours, shard_lines)
    line_gradient = (
        lax.psum_scatter(
            line_sum.reshape(1, hours, shard_lines), "ctg", scatter_dimension=2, tiled=True
        )
        / outages
    )
    outage_local = outage_part.transpose(1, 0, 2).reshape(hours, kblocks * tile)
    outage_gradient = lax.psum(outage_local, "line") * outage_scale
    return (updated, line_gradient, outage_gradient)


def solution(mesh):
    placed = (
        P("line", "grp", "ctg"),
        P("line"),
        P("ctg", "line", None, None),
        P("ctg", "line"),
        P("ctg"),
        P(),
        P("ctg", "line", "grp", None, None),
    )
    return jax.shard_map(
        per_device,
        mesh=mesh,
        in_specs=placed,
        out_specs=(P("ctg", "line", "grp", None, None), P("line", "grp", "ctg"), P("grp", "ctg")),
        check_vma=False,
    )
```

profile of v0, /device:TPU:0, one launch (start us, length us, event | category | flops | bytes accessed | tf_op | source)
XLA Modules:
  0.0 172.5 jit_solution(10585208698374623143)
XLA Ops:
  7.2 0.0 copy-start
  7.2 0.0 reduce-scatter.4.cloned.1.call-start
  7.2 0.7 compare_and_fusion
  7.9 0.7 compare_select_fusion
  8.6 0.7 compare_select_fusion.2
  9.2 0.6 scatter_custom_fusion
  9.8 0.8 convert_reduce_fusion
  10.6 0.8 copy.30
  11.5 1.0 bitcast_convert_fusion
  12.5 26.8 %all_gather.3 = f32[16,12,1280]{2,1,0:T(8,128)S(1)} all-gather(f32[1,12,1280]{2,1,0:T(8,128)S(1)} %copy.30), channel_id=1, replica_groups=mesh['grp'=2,'ctg'=4,'line'=4] {'ctg','line'}, dimensions={0}, use_global_device_ids=true | all-gather | bytes 1044480 | tf_op jit(solution)/shard_map/all_gather | solution.py:41
  39.2 0.6 copy.32
  39.9 1.1 gather_fusion
  41.0 0.3 select_bitcast_fusion
  41.3 0.6 copy.33
  41.9 0.5 reshape.232
  42.5 0.0 copy-start.2
  42.5 5.5 %copy.35 = f32[12,20480]{0,1:T(8,128)} copy(f32[12,20480]{1,0:T(8,128)S(1)} %reshape.232) | data formatting | bytes 1966080 | tf_op jit(solution)/shard_map/reshape | solution.py:43
  48.0 0.1 copy.42
  48.1 0.0 copy-done.2
  48.1 0.2 fusion.3
  48.3 4.6 %gather_fusion.1 = f32[128,12]{1,0:T(8,128)S(1)} fusion(f32[12,20480]{0,1:T(8,128)} %copy.35, s32[1024]{0:T(1024)S(1)} %pad_clamp_fusion), kind=kCustom, calls=%fused_computation.1 | custom fusion | bytes 12800 | tf_op jit(solution)/shard_map/jit(_take)/gather | solution.py:47
  52.9 0.1 select_bitcast_fusion.1
  53.0 0.1 copy.36
  53.1 0.0 copy-done
  53.1 0.1 fusion.2
  53.2 7.3 %multiply_reduce_fusion = (f32[12,128]{1,0:T(8,128)S(1)}, f32[8,12,128]{2,1,0:T(8,128)S(1)}, f32[1,8,12,128,128]{4,3,2,1,0:T(8,128)}) fusion(f32[8,128]{1,0:T(8,128)S(1)} %fusion.2, f32[12,128]{1,0:T(8,128)S(1)} %copy.36, f32[8,128,128]{2,1,0:T(8,128)S(1)} %bitcast_convert_fusion, f32[8,12,128]{2,1,0:T(8,128)S(1)} %copy.34, f32[8]{0:T(128)S(1)} %convert_reduce_fusion, ...), kind=kLoop, calls=%fused_computation.5 | loop fusion | flops 22006272 | bytes 13221920 | tf_op jit(solution)/shard_map/vmap()/reduce_sum | solution.py:25
  60.5 0.3 fusion.5
  60.8 19.8 %copy.40 = f32[1,12,5120]{0,1,2:T(8,128)} copy(f32[1,12,5120]{2,0,1:T(1,128)S(1)} %bitcast.39) | data formatting | bytes 491520
  80.5 20.4 %bitcast_reduce_fusion = f32[5120,12]{1,0:T(8,128)} fusion(f32[1,12,5120]{0,1,2:T(8,128)} %copy.40), kind=kLoop, calls=%fused_computation.3 | loop fusion | bytes 491520
  101.0 0.0 reduce-scatter.4.cloned.1.call-update
  101.0 6.1 %psum.7 = f32[12,128]{1,0:T(8,128)S(1)} all-reduce(f32[12,128]{1,0:T(8,128)S(1)} %get-tuple-element.3), channel_id=1, replica_groups=mesh['grp'=2,'ctg'=4,'line'=4] {'line'}, use_global_device_ids=true, to_apply=%region_5.6 | all-reduce | flops 1536 | bytes 12288 | tf_op jit(solution)/shard_map/psum | solution.py:62
  107.1 0.6 broadcast_multiply_fusion.1
  107.7 43.0 %reduce-scatter.4.cloned.1.call-done = f32[1280,12]{1,0:T(8,128)} async-done(((f32[5120,12]{1,0:T(8,128)}), f32[1280,12]{1,0:T(8,128)}) %reduce-scatter.4.cloned.1.call-update) | async-done | bytes 61456
  150.8 0.0 copy-start.1
  150.8 8.2 %reshape_bitcast_fusion = f32[1,12,1280]{0,1,2:T(8,128)} fusion(f32[1280,12]{1,0:T(8,128)} %reduce-scatter.4.cloned.1.call-done), kind=kLoop, calls=%fused_computation.4 | loop fusion | bytes 122880
  158.9 6.0 %copy.41 = f32[1,12,1280]{2,0,1:T(1,128)S(1)} copy(f32[1,12,1280]{0,1,2:T(8,128)} %reshape_bitcast_fusion) | data formatting | bytes 122880
  165.0 0.7 broadcast_multiply_fusion
  165.6 0.0 copy-done.1
  (8 shorter events, 0.1 us)
Async XLA Ops:
  7.2 45.9 %copy-start = (f32[5120]{0:T(1024)S(1)}, f32[5120]{0:T(1024)}, u32[]{:S(2)}) copy-start(f32[5120]{0:T(1024)} %param.8) | copy-start | bytes 61444
  7.2 143.6 %reduce-scatter.4.cloned.1.call-start = ((), (), s32[]{:S(2)}) async-start(), calls=%async_computation.1 | async-start | bytes 3276800
  42.5 5.6 %copy-start.2 = (s32[1,40]{1,0:T(1,128)S(1)}, s32[1,40]{1,0:T(1,128)}, u32[]{:S(2)}) copy-start(s32[1,40]{1,0:T(1,128)} %param.10) | copy-start | bytes 484
  150.8 14.9 %copy-start.1 = (f32[5120]{0:T(1024)S(1)}, f32[5120]{0:T(1024)}, u32[]{:S(2)}) copy-start(f32[5120]{0:T(1024)} %param.8) | copy-start | bytes 61444
Sparse Core Ops, SparseCore 0:
  101.1 49.6 reduce-scatter.3
where the time goes:
time: 173 us; the launch traced here: 172 us
  local copies, waits for them, and re-layouts  69 us (40%)
  waiting for transfers between devices  43.1 us (25%)
  blocking collectives  32.9 us (19%)
  between operations  14.2 us (8%)
  other arithmetic  12.7 us (7%)
    unnamed x12, local copies, waits for them, and re-layouts  55.3 us
    unnamed x2, waiting for transfers between devices  43.1 us
    all_gather x1, blocking collectives, per_device(): gathered = lax.all_gather(owned_flow, ('ctg', 'line'), axis=0, tiled=True)  26.8 us
    reduce_sum x1, other arithmetic, tile_step(): outage_part = jnp.sum(lodf[:, None, :, :] * weight, axis=(0, 3))  7.34 us
    psum x1, blocking collectives, per_device(): outage_gradient = lax.psum(outage_local, 'line') * outage_scale  6.12 us
    reshape x2, local copies, waits for them, and re-layouts, per_device(): shaped.transpose(2, 1, 0, 3).reshape(hours, line_count * shard_lines)  5.99 us
    gather x1, local copies, waits for them, and re-layouts, per_device(): outage_flow = jnp.take(every_flow, outage_line, axis=1)  4.62 us
  transfers between devices with their start and end apart: 1, of which 1 were waited for; matrix products, arithmetic and copies ran while one was open for 0% of the time, Pallas kernels for 0%

commit v1 on v0

--- a/solution.py
+++ b/solution.py
@@ -1,10 +1,17 @@
+import functools
+
 import jax
 import jax.numpy as jnp
 from jax import lax
+from jax.experimental import pallas as pl
+from jax.experimental.pallas import tpu as pltpu
 from jax.sharding import PartitionSpec as P
 
 dual_step = 0.5
 outage_scale = 0.0625
+MESH = pl.DeviceIdType.MESH
+LANES = 128
+ROWS = 8
 
 
 def tile_step(tiles, slot_map, flow_rows, rating_rows, outage_flow, multipliers):
@@ -26,7 +33,7 @@
     return (updated, line_part, outage_part)
 
 
-def per_device(owned_flow, ratings, lodf_tiles, tile_map, outage_line, block_owner, multipliers):
+def per_device_general(owned_flow, ratings, lodf_tiles, tile_map, outage_line, block_owner, multipliers):
     hours = owned_flow.shape[1]
     piece = owned_flow.shape[2]
     ctg_count = lax.axis_size("ctg")
@@ -63,6 +70,327 @@
     return (updated, line_gradient, outage_gradient)
 
 
+def kernel(
+    n_ctg, n_line, outages,
+    map_hbm, owner_hbm, outage_hbm, rating_hbm, own_hbm, lodf_hbm, mult_hbm,
+    new_ref, line_ref, grad_ref,
+    map_ref, owner_ref, outage_ref, rating_ref,
+    mult, lodf16, lodf, flows, onehot, slot_flow, slot_half, slot_bar, spread, acc, direct,
+    map_send, map_recv, part, grad,
+    small_sem, mult_sem, lodf_sem, own_sem, flow_ssem, flow_rsem, map_ssem, map_rsem,
+    part_ssem, part_rsem, dir_ssem, dir_rsem, grad_ssem, grad_rsem,
+):
+    slots, hours, tile, _ = mult.shape
+    inner = flows.shape[1] // hours
+    piece = inner * tile
+    me_c = lax.axis_index("ctg")
+    me_l = lax.axis_index("line")
+
+    def other_c(d):
+        return lax.rem(me_c + d, n_ctg)
+
+    def other_l(d):
+        return lax.rem(me_l + d, n_line)
+
+    barrier = pltpu.get_barrier_semaphore()
+    for d in range(1, n_ctg):
+        pl.semaphore_signal(barrier, inc=1, device_id={"ctg": other_c(d)}, device_id_type=MESH)
+    for d in range(1, n_line):
+        pl.semaphore_signal(barrier, inc=1, device_id={"line": other_l(d)}, device_id_type=MESH)
+
+    own_copy = pltpu.make_async_copy(own_hbm, flows.at[me_c], own_sem)
+    own_copy.start()
+    small_copies = [
+        pltpu.make_async_copy(src, dst, small_sem.at[i])
+        for i, (src, dst) in enumerate(
+            ((map_hbm, map_ref), (owner_hbm, owner_ref), (outage_hbm, outage_ref), (rating_hbm, rating_ref))
+        )
+    ]
+    for copy in small_copies:
+        copy.start()
+    lodf_copy = pltpu.make_async_copy(lodf_hbm.at[0], lodf16, lodf_sem)
+    lodf_copy.start()
+    for s in range(slots):
+        pltpu.make_async_copy(mult_hbm.at[0, s], mult.at[s], mult_sem.at[s]).start()
+
+    for copy in small_copies:
+        copy.wait()
+    for q in range(n_ctg):
+        for i in range(inner):
+            map_send[q, pl.ds(i, 1), :] = jnp.full((1, LANES), map_ref[0, q * inner + i], jnp.int32)
+    own_copy.wait()
+    pl.semaphore_wait(barrier, n_ctg - 1 + n_line - 1)
+
+    flow_copies = []
+    for d in range(1, n_ctg):
+        copy = pltpu.make_async_remote_copy(
+            src_ref=flows.at[me_c], dst_ref=flows.at[me_c],
+            send_sem=flow_ssem.at[d], recv_sem=flow_rsem.at[d],
+            device_id={"ctg": other_c(d)}, device_id_type=MESH,
+        )
+        copy.start()
+        flow_copies.append(copy)
+    map_copies = []
+    for d in range(1, n_ctg):
+        copy = pltpu.make_async_remote_copy(
+            src_ref=map_send.at[other_c(d)], dst_ref=map_recv.at[me_c],
+            send_sem=map_ssem.at[d], recv_sem=map_rsem.at[d],
+            device_id={"ctg": other_c(d)}, device_id_type=MESH,
+        )
+        copy.start()
+        map_copies.append(copy)
+    map_recv[me_c] = map_send[me_c]
+
+    rows_iota = lax.broadcasted_iota(jnp.int32, (tile, LANES), 0)
+    for c in range(n_ctg):
+        base = (me_l * n_ctg + owner_ref[c]) * piece
+        wanted = jnp.broadcast_to(outage_ref[...] - base, (tile, LANES))
+
+        def hot_body(b, carry, c=c, wanted=wanted):
+            row = pl.multiple_of(b * tile, tile)
+            hit = (rows_iota + row) == wanted
+            onehot[c, pl.ds(row, tile), :] = jnp.where(hit, 1.0, 0.0).astype(jnp.bfloat16)
+            return carry
+
+        lax.fori_loop(0, inner, hot_body, 0)
+
+    slot_iota = lax.broadcasted_iota(jnp.int32, (slots, LANES), 0)
+    rating = jnp.ones((slots, LANES), jnp.float32)
+    there = jnp.zeros((slots, LANES), jnp.float32)
+    for b in range(n_ctg * inner):
+        hit = slot_iota == map_ref[0, b]
+        rating = jnp.where(hit, jnp.broadcast_to(rating_ref[pl.ds(b, 1), :], (slots, LANES)), rating)
+        there = jnp.where(hit, 1.0, there)
+    slot_half[...] = there * (dual_step / (rating * rating))
+    slot_bar[...] = jnp.where(there > 0.0, dual_step, 1e30)
+
+    lodf_copy.wait()
+
+    def lodf_body(s, carry):
+        lodf[s] = lodf16[s].astype(jnp.float32)
+        return carry
+
+    lax.fori_loop(0, slots, lodf_body, 0)
+    acc[...] = jnp.zeros_like(acc)
+
+    def pick(c):
+        value = jnp.concatenate(
+            [flows[c, pl.ds(i, hours, stride=inner), :] for i in range(inner)], axis=1
+        )
+        high = value.astype(jnp.bfloat16)
+        rest = value - high.astype(jnp.float32)
+        middle = rest.astype(jnp.bfloat16)
+        low = (rest - middle.astype(jnp.float32)).astype(jnp.bfloat16)
+        table = onehot[c]
+        total = jnp.dot(high, table, preferred_element_type=jnp.float32)
+        total = total + jnp.dot(middle, table, preferred_element_type=jnp.float32)
+        return total + jnp.dot(low, table, preferred_element_type=jnp.float32)
+
+    def place(c, found):
+        hits = []
+        for i in range(inner):
+            block = jnp.int32(-1)
+            for q in range(n_ctg):
+                block = jnp.where(owner_ref[c] == q, map_ref[0, q * inner + i], block)
+            hits.append(slot_iota == block)
+        out = []
+        for t in range(hours):
+            rows = found[t]
+            for i in range(inner):
+                row = flows[c, pl.ds(t * inner + i, 1), :]
+                rows = jnp.where(hits[i], jnp.broadcast_to(row, (slots, LANES)), rows)
+            out.append(rows)
+        return out
+
+    order = [me_c]
+    picked = pick(me_c)
+    for d in (1, 3, 2) if n_ctg == 4 else range(1, n_ctg):
+        flow_copies[d - 1].wait_recv()
+        order.append(lax.rem(me_c + n_ctg - d, n_ctg))
+        picked = picked + pick(order[-1])
+    part[me_l] = picked
+    part_copies = []
+    for d in range(1, n_line):
+        copy = pltpu.make_async_remote_copy(
+            src_ref=part.at[me_l], dst_ref=part.at[me_l],
+            send_sem=part_ssem.at[d], recv_sem=part_rsem.at[d],
+            device_id={"line": other_l(d)}, device_id_type=MESH,
+        )
+        copy.start()
+        part_copies.append(copy)
+
+    found = [jnp.zeros((slots, LANES), jnp.float32)] * hours
+    for c in range(n_ctg):
+        found = place(c, found)
+    for t in range(hours):
+        slot_flow[t] = found[t]
+
+    for copy in part_copies:
+        copy.wait_recv()
+    outage = part[0]
+    for j in range(1, n_line):
+        outage = outage + part[j]
+    turned = jnp.concatenate([outage, jnp.zeros((16 - hours, LANES), jnp.float32)], axis=0).T
+    for t in range(hours):
+        spread[t] = jnp.broadcast_to(turned[:, t : t + 1], (tile, LANES))
+
+    def direct_copy(s, d):
+        return pltpu.make_async_remote_copy(
+            src_ref=direct.at[me_c, s], dst_ref=direct.at[me_c, s],
+            send_sem=dir_ssem.at[s, d], recv_sem=dir_rsem.at[s, d],
+            device_id={"ctg": other_c(d)}, device_id_type=MESH,
+        )
+
+    def slot_body(s, carry):
+        pltpu.make_async_copy(mult_hbm.at[0, s], mult.at[s], mult_sem.at[s]).wait()
+        half = jnp.broadcast_to(slot_half[pl.ds(s, 1), :], (ROWS, LANES))
+        bar = jnp.broadcast_to(slot_bar[pl.ds(s, 1), :], (ROWS, LANES))
+        base = [
+            jnp.broadcast_to(slot_flow[t, pl.ds(s, 1), :], (ROWS, LANES)) for t in range(hours)
+        ]
+
+        def row_body(k, sums):
+            row = pl.multiple_of(k * ROWS, ROWS)
+            factor = lodf[s, pl.ds(row, ROWS), :]
+            out = []
+            for t in range(hours):
+                post = base[t] + factor * spread[t, pl.ds(row, ROWS), :]
+                scaled = post * half
+                updated = jnp.maximum(mult[s, t, pl.ds(row, ROWS), :] + (post * scaled - bar), 0.0)
+                new_ref[s, t, pl.ds(row, ROWS), :] = updated
+                weight = updated * scaled
+                acc[t, pl.ds(row, ROWS), :] += factor * weight
+                out.append(sums[t] + weight)
+            return tuple(out)
+
+        zero = jnp.zeros((ROWS, LANES), jnp.float32)
+        sums = lax.fori_loop(0, tile // ROWS, row_body, (zero,) * hours)
+        for t in range(hours):
+            direct[me_c, s, pl.ds(t, 1), :] = jnp.sum(sums[t], axis=0, keepdims=True)
+        for d in range(1, n_ctg):
+            direct_copy(s, d).start()
+        return carry
+
+    lax.fori_loop(0, slots, slot_body, 0)
+
+    columns = lax.broadcasted_iota(jnp.int32, (tile, LANES), 1)
+    packed = jnp.zeros((tile, LANES), jnp.float32)
+    for t in range(hours):
+        packed = jnp.where(columns == t, jnp.sum(acc[t], axis=1, keepdims=True), packed)
+    grad[me_l] = packed.T[:hours]
+    grad_copies = []
+    for d in range(1, n_line):
+        copy = pltpu.make_async_remote_copy(
+            src_ref=grad.at[me_l], dst_ref=grad.at[me_l],
+            send_sem=grad_ssem.at[d], recv_sem=grad_rsem.at[d],
+            device_id={"line": other_l(d)}, device_id_type=MESH,
+        )
+        copy.start()
+        grad_copies.append(copy)
+
+    for copy in map_copies:
+        copy.wait_recv()
+
+    def direct_wait(s, carry):
+        for d in range(1, n_ctg):
+            direct_copy(s, d).wait()
+        return carry
+
+    lax.fori_loop(0, slots, direct_wait, 0)
+
+    for i in range(inner):
+        total = jnp.zeros((hours, LANES), jnp.float32)
+        for c in range(n_ctg):
+            which = jnp.broadcast_to(map_recv[c, pl.ds(i, 1), :], (hours, LANES))
+            found = jnp.zeros((hours, LANES), jnp.float32)
+            for s in range(slots):
+                found = jnp.where(which == s, direct[c, s], found)
+            total = total + found
+        line_ref[pl.ds(i, hours, stride=inner), :] = total * (1.0 / dual_step / outages)
+
+    for copy in grad_copies:
+        copy.wait_recv()
+    total = grad[0]
+    for j in range(1, n_line):
+        total = total + grad[j]
+    grad_ref[...] = total * (outage_scale / dual_step)
+
+    for copy in flow_copies + map_copies + part_copies + grad_copies:
+        copy.wait_send()
+
+
+def per_device_fused(owned_flow, ratings, lodf_tiles, tile_map, outage_line, block_owner, multipliers):
+    n_ctg = lax.axis_size("ctg")
+    n_line = lax.axis_size("line")
+    _, hours, piece = owned_flow.shape
+    _, slots, tile, _ = lodf_tiles.shape
+    inner = piece // tile
+    outages = outage_line.shape[0] * n_ctg
+    f32, bf16, i32 = jnp.float32, jnp.bfloat16, jnp.int32
+    dma = pltpu.SemaphoreType.DMA
+    vmem = pl.BlockSpec(memory_space=pltpu.VMEM)
+    hbm = pl.BlockSpec(memory_space=pltpu.HBM)
+    updated, line_gradient, outage_gradient = pl.pallas_call(
+        functools.partial(kernel, n_ctg, n_line, outages),
+        out_shape=(
+            jax.ShapeDtypeStruct((slots, hours, tile, tile), f32),
+            jax.ShapeDtypeStruct((hours * inner, tile), f32),
+            jax.ShapeDtypeStruct((hours, tile), f32),
+        ),
+        in_specs=[hbm] * 7,
+        out_specs=(vmem, vmem, vmem),
+        scratch_shapes=[
+            pltpu.SMEM(tile_map.shape, i32),
+            pltpu.SMEM(block_owner.shape, i32),
+            pltpu.VMEM((1, tile), i32),
+            pltpu.VMEM((n_ctg * inner, tile), f32),
+            pltpu.VMEM((slots, hours, tile, tile), f32),
+            pltpu.VMEM((slots, tile, tile), bf16),
+            pltpu.VMEM((slots, tile, tile), f32),
+            pltpu.VMEM((n_ctg, hours * inner, tile), f32),
+            pltpu.VMEM((n_ctg, piece, tile), bf16),
+            pltpu.VMEM((hours, slots, tile), f32),
+            pltpu.VMEM((slots, tile), f32),
+            pltpu.VMEM((slots, tile), f32),
+            pltpu.VMEM((hours, tile, tile), f32),
+            pltpu.VMEM((hours, tile, tile), f32),
+            pltpu.VMEM((n_ctg, slots, hours, tile), f32),
+            pltpu.VMEM((n_ctg, inner, tile), i32),
+            pltpu.VMEM((n_ctg, inner, tile), i32),
+            pltpu.VMEM((n_line, hours, tile), f32),
+            pltpu.VMEM((n_line, hours, tile), f32),
+            dma((4,)), dma((slots,)), dma, dma,
+            dma((n_ctg,)), dma((n_ctg,)), dma((n_ctg,)), dma((n_ctg,)),
+            dma((n_line,)), dma((n_line,)),
+            dma((slots, n_ctg)), dma((slots, n_ctg)),
+            dma((n_line,)), dma((n_line,)),
+        ],
+        compiler_params=pltpu.CompilerParams(
+            collective_id=0, has_side_effects=True, vmem_limit_bytes=40 * 1024 * 1024
+        ),
+        name="dual_step",
+    )(
+        tile_map, block_owner, outage_line.reshape(1, tile), ratings.reshape(n_ctg * inner, tile),
+        owned_flow.reshape(hours * inner, tile), lodf_tiles, multipliers,
+    )
+    return updated[None], line_gradient.reshape(1, hours, piece), outage_gradient
+
+
+def per_device(owned_flow, ratings, lodf_tiles, tile_map, outage_line, block_owner, multipliers):
+    n_ctg = lax.axis_size("ctg")
+    tile = lodf_tiles.shape[-1]
+    whole = (
+        tile == LANES
+        and owned_flow.shape[1] <= 16
+        and owned_flow.shape[2] % tile == 0
+        and outage_line.shape[0] == tile
+        and lodf_tiles.shape[0] == 1
+        and n_ctg <= 4
+    )
+    form = per_device_fused if whole else per_device_general
+    return form(owned_flow, ratings, lodf_tiles, tile_map, outage_line, block_owner, multipliers)
+
+
 def solution(mesh):
     placed = (
         P("line", "grp", "ctg"),

time: 173 us -> 36.6 us (0.21)
  local copies, waits for them, and re-layouts: 69 us -> 11.2 us
  waiting for transfers between devices: 43.1 us -> 0 us
  blocking collectives: 32.9 us -> 0 us
  Pallas kernels: 0 us -> 24.5 us
  between operations: 14.2 us -> 0.66 us
  other arithmetic: 12.7 us -> 0 us
    unnamed x12 -> x17, local copies, waits for them, and re-layouts: 55.3 us -> 11.2 us
    unnamed x2 -> x0, waiting for transfers between devices: 43.1 us -> none
    all_gather x1 -> x0, blocking collectives: 26.8 us -> none  [per_device(): gathered = lax.all_gather(owned_flow, ('ctg', 'line'), axis=0, tiled=True)]
    pallas_call x0 -> x1, Pallas kernels: none -> 24.5 us  [per_device_fused(): pl.pallas_call(functools.partial(kernel, n_ctg, n_line, outages), out_sha...]
    reduce_sum x2 -> x0, other arithmetic: 8.11 us -> none  [the longest x1 7.34 us: tile_step(): outage_part = jnp.sum(lodf[:, None, :, :] * weight, axis=(0, 3))]
    reshape x3 -> x0, local copies, waits for them, and re-layouts: 6.62 us -> none  [the longest x2 5.99 us: per_device(): shaped.transpose(2, 1, 0, 3).reshape(hours, line_count * shard_lines)]
    psum x1 -> x0, blocking collectives: 6.12 us -> none  [per_device(): outage_gradient = lax.psum(outage_local, 'line') * outage_scale]
    gather x2 -> x0, local copies, waits for them, and re-layouts: 5.76 us -> none  [the longest x1 4.62 us: per_device(): outage_flow = jnp.take(every_flow, outage_line, axis=1)]
  transfers between devices with their start and end apart: 1 -> 0, of which waited for: 1 -> 0; matrix products, arithmetic and copies ran while one was open for 0% -> 0% of each run, Pallas kernels for 0% -> 0%
where the time goes in v1:
time: 36.6 us; the launch traced here: 36.3 us
  Pallas kernels  24.5 us (67%)
  local copies, waits for them, and re-layouts  11.2 us (31%)
  between operations  0.66 us (2%)
    pallas_call x1, Pallas kernels, per_device_fused(): pl.pallas_call(functools.partial(kernel, n_ctg, n_line, outages), out_sha...  24.5 us
    unnamed x17, local copies, waits for them, and re-layouts  11.2 us

profile of v1, /device:TPU:0, one launch (start us, length us, event | category | flops | bytes accessed | tf_op | source)
XLA Modules:
  0.0 36.3 jit_solution(3361466512766084087)
XLA Ops:
  0.6 0.0 copy-start
  0.6 2.8 %copy-done = f32[1,8,12,128,128]{4,3,2,1,0:T(8,128)S(1)} copy-done((f32[1,8,12,128,128]{4,3,2,1,0:T(8,128)S(1)}, f32[1,8,12,128,128]{4,3,2,1,0:T(8,128)}, u32[]{:S(2)}) %copy-start) | copy-done | bytes 6291480
  3.4 0.0 copy-start.1
  3.4 0.9 %copy-done.1 = bf16[1,8,128,128]{3,2,1,0:T(8,128)(2,1)S(1)} copy-done((bf16[1,8,128,128]{3,2,1,0:T(8,128)(2,1)S(1)}, bf16[1,8,128,128]{3,2,1,0:T(8,128)(2,1)}, u32[]{:S(2)}) %copy-start.1) | copy-done | bytes 262168
  4.4 0.0 copy-start.2
  4.4 0.8 %copy-done.2 = f32[1,12,1280]{2,0,1:T(1,128)S(1)} copy-done((f32[1,12,1280]{2,0,1:T(1,128)S(1)}, f32[1,12,1280]{2,0,1:T(1,128)}, u32[]{:S(2)}) %copy-start.2) | copy-done | bytes 61464
  5.2 0.0 copy-start.3
  5.2 0.7 %copy-done.3 = f32[5120]{0:T(1024)S(1)} copy-done((f32[5120]{0:T(1024)S(1)}, f32[5120]{0:T(1024)}, u32[]{:S(2)}) %copy-start.3) | copy-done | bytes 20504
  5.9 0.0 copy-start.4
  5.9 0.7 %copy-done.4 = s32[1,40]{1,0:T(1,128)S(1)} copy-done((s32[1,40]{1,0:T(1,128)S(1)}, s32[1,40]{1,0:T(1,128)}, u32[]{:S(2)}) %copy-start.4) | copy-done | bytes 184
  6.6 0.0 copy-start.5
  6.6 0.7 %copy-done.5 = s32[4]{0:T(128)S(1)} copy-done((s32[4]{0:T(128)S(1)}, s32[4]{0:T(128)}, u32[]{:S(2)}) %copy-start.5) | copy-done | bytes 40
  7.2 0.0 copy-start.6
  7.2 0.7 %copy-done.6 = s32[128]{0:T(128)S(1)} copy-done((s32[128]{0:T(128)S(1)}, s32[128]{0:T(128)}, u32[]{:S(2)}) %copy-start.6) | copy-done | bytes 536
  7.9 24.5 %dual_step.1 = (f32[8,12,128,128]{3,2,1,0:T(8,128)S(1)}, f32[120,128]{1,0:T(8,128)S(1)}, f32[12,128]{1,0:T(8,128)S(1)}) custom-call(s32[1,40]{1,0:T(1,128)S(1)} %copy-done.4, s32[4]{0:T(128)S(1)} %copy-done.5, s32[1,128]{1,0:T(1,128)S(1)} %bitcast.9, f32[40,128]{1,0:T(8,128)S(1)} %bitcast.8, f32[120,128]{1,0:T(8,128)S(1)} %bitcast.7, ...), custom_call_target="tpu_custom_call" | custom-call | tf_op jit(solution)/shard_map/dual_step/pallas_call | solution.py:333
  32.4 2.7 %copy.15 = f32[1,8,12,128,128]{4,3,2,1,0:T(8,128)} copy(f32[1,8,12,128,128]{4,3,2,1,0:T(8,128)S(1)} %bitcast.5) | data formatting | bytes 12582912
  35.1 0.6 %copy.16 = f32[1,12,1280]{2,0,1:T(1,128)} copy(f32[1,12,1280]{2,0,1:T(1,128)S(1)} %bitcast.6) | data formatting | bytes 122880
  35.7 0.6 %copy.17 = f32[12,128]{1,0:T(8,128)} copy(f32[12,128]{1,0:T(8,128)S(1)} %get-tuple-element.20) | data formatting | bytes 12288
Async XLA Ops:
  0.6 2.8 %copy-start = (f32[1,8,12,128,128]{4,3,2,1,0:T(8,128)S(1)}, f32[1,8,12,128,128]{4,3,2,1,0:T(8,128)}, u32[]{:S(2)}) copy-start(f32[1,8,12,128,128]{4,3,2,1,0:T(8,128)} %mult_hbm.1) | copy-start | bytes 18874372
  3.4 0.9 %copy-start.1 = (bf16[1,8,128,128]{3,2,1,0:T(8,128)(2,1)S(1)}, bf16[1,8,128,128]{3,2,1,0:T(8,128)(2,1)}, u32[]{:S(2)}) copy-start(bf16[1,8,128,128]{3,2,1,0:T(8,128)(2,1)} %lodf_hbm.1) | copy-start | bytes 786436
  4.4 0.8 %copy-start.2 = (f32[1,12,1280]{2,0,1:T(1,128)S(1)}, f32[1,12,1280]{2,0,1:T(1,128)}, u32[]{:S(2)}) copy-start(f32[1,12,1280]{2,0,1:T(1,128)} %param.7) | copy-start | bytes 184324
  5.2 0.7 %copy-start.3 = (f32[5120]{0:T(1024)S(1)}, f32[5120]{0:T(1024)}, u32[]{:S(2)}) copy-start(f32[5120]{0:T(1024)} %param.8) | copy-start | bytes 61444
  5.9 0.7 %copy-start.4 = (s32[1,40]{1,0:T(1,128)S(1)}, s32[1,40]{1,0:T(1,128)}, u32[]{:S(2)}) copy-start(s32[1,40]{1,0:T(1,128)} %map_hbm.1) | copy-start | bytes 484
  6.6 0.7 %copy-start.5 = (s32[4]{0:T(128)S(1)}, s32[4]{0:T(128)}, u32[]{:S(2)}) copy-start(s32[4]{0:T(128)} %owner_hbm.1) | copy-start | bytes 52
  7.2 0.7 %copy-start.6 = (s32[128]{0:T(128)S(1)}, s32[128]{0:T(128)}, u32[]{:S(2)}) copy-start(s32[128]{0:T(128)} %param.11) | copy-start | bytes 1540

commit v2 on v1

--- a/solution.py
+++ b/solution.py
@@ -366,7 +366,7 @@
             dma((n_line,)), dma((n_line,)),
         ],
         compiler_params=pltpu.CompilerParams(
-            collective_id=0, has_side_effects=True, vmem_limit_bytes=40 * 1024 * 1024
+            collective_id=0, has_side_effects=True, vmem_limit_bytes=62 * 1024 * 1024
         ),
         name="dual_step",
     )(

time: 36.6 us -> 35.8 us (0.978)
  local copies, waits for them, and re-layouts: 11.2 us -> 7.54 us
  Pallas kernels: 24.5 us -> 27.4 us
    unnamed x17 -> x7, local copies, waits for them, and re-layouts: 11.2 us -> 7.54 us
    pallas_call x1, Pallas kernels: 24.5 us -> 27.4 us  [per_device_fused(): pl.pallas_call(functools.partial(kernel, n_ctg, n_line, outages), out_sha...]
where the time goes in v2:
time: 35.8 us; the launch traced here: 35.6 us
  Pallas kernels  27.4 us (77%)
  local copies, waits for them, and re-layouts  7.54 us (21%)
  between operations  0.66 us (2%)
    pallas_call x1, Pallas kernels, per_device_fused(): pl.pallas_call(functools.partial(kernel, n_ctg, n_line, outages), out_sha...  27.4 us
    unnamed x7, local copies, waits for them, and re-layouts  7.54 us

profile of v2, /device:TPU:0, one launch (start us, length us, event | category | flops | bytes accessed | tf_op | source)
XLA Modules:
  0.0 35.6 jit_solution(7397522371206737351)
XLA Ops:
  0.6 27.4 %dual_step.1 = (f32[8,12,128,128]{3,2,1,0:T(8,128)}, f32[120,128]{1,0:T(8,128)}, f32[12,128]{1,0:T(8,128)}) custom-call(s32[1,40]{1,0:T(1,128)} %map_hbm.1, s32[4]{0:T(128)} %owner_hbm.1, s32[1,128]{1,0:T(1,128)} %bitcast.9, f32[40,128]{1,0:T(8,128)} %bitcast.8, f32[120,128]{1,0:T(8,128)} %bitcast.7, bf16[1,8,128,128]{3,2,1,0:T(8,128)(2,1)} %lodf_hbm.1, ...), custom_call_target="tpu_custom_call" | custom-call | tf_op jit(solution)/shard_map/dual_step/pallas_call | solution.py:333
  28.1 0.0 copy-start
  28.1 0.0 copy-start.1
  28.1 6.3 %copy.15 = f32[1,8,12,128,128]{4,3,2,1,0:T(8,128)} copy(f32[1,8,12,128,128]{4,3,2,1,0:T(8,128)} %bitcast.5) | data formatting | bytes 12582912
  34.4 0.0 copy-done
  34.4 0.6 %copy.16 = f32[1,12,1280]{2,0,1:T(1,128)} copy(f32[1,12,1280]{2,0,1:T(1,128)S(1)} %bitcast.6) | data formatting | bytes 122880
  35.0 0.0 copy-done.1
  35.0 0.6 %copy.17 = f32[12,128]{1,0:T(8,128)} copy(f32[12,128]{1,0:T(8,128)S(1)} %copy-done.1) | data formatting | bytes 12288
Async XLA Ops:
  28.1 6.3 %copy-start = (f32[120,128]{1,0:T(8,128)S(1)}, f32[120,128]{1,0:T(8,128)}, u32[]{:S(2)}) copy-start(f32[120,128]{1,0:T(8,128)} %get-tuple-element.7) | copy-start | bytes 184324
  28.1 6.9 %copy-start.1 = (f32[12,128]{1,0:T(8,128)S(1)}, f32[12,128]{1,0:T(8,128)}, u32[]{:S(2)}) copy-start(f32[12,128]{1,0:T(8,128)} %get-tuple-element.20) | copy-start | bytes 18436

commit v3 on v1

--- a/solution.py
+++ b/solution.py
@@ -370,8 +370,14 @@
         ),
         name="dual_step",
     )(
-        tile_map, block_owner, outage_line.reshape(1, tile), ratings.reshape(n_ctg * inner, tile),
-        owned_flow.reshape(hours * inner, tile), lodf_tiles, multipliers,
+        *(
+            pltpu.with_memory_space_constraint(x, pltpu.HBM)
+            for x in (
+                tile_map, block_owner, outage_line.reshape(1, tile),
+                ratings.reshape(n_ctg * inner, tile), owned_flow.reshape(hours * inner, tile),
+                lodf_tiles, multipliers,
+            )
+        )
     )
     return updated[None], line_gradient.reshape(1, hours, piece), outage_gradient
 

time: 36.6 us -> 29.5 us (0.81)
  local copies, waits for them, and re-layouts: 11.2 us -> 3.93 us
    unnamed x17 -> x3, local copies, waits for them, and re-layouts: 11.2 us -> 3.93 us
where the time goes in v3:
time: 29.5 us; the launch traced here: 29.3 us
  Pallas kernels  24.8 us (84%)
  local copies, waits for them, and re-layouts  3.93 us (13%)
  between operations  0.64 us (2%)
    pallas_call x1, Pallas kernels, per_device_fused(): pl.pallas_call(functools.partial(kernel, n_ctg, n_line, outages), out_sha...  24.8 us
    unnamed x3, local copies, waits for them, and re-layouts  3.93 us

profile of v3, /device:TPU:0, one launch (start us, length us, event | category | flops | bytes accessed | tf_op | source)
XLA Modules:
  0.0 29.3 jit_solution(15884263328025370169)
XLA Ops:
  0.6 24.8 %dual_step.1 = (f32[8,12,128,128]{3,2,1,0:T(8,128)S(1)}, f32[120,128]{1,0:T(8,128)S(1)}, f32[12,128]{1,0:T(8,128)S(1)}) custom-call(s32[1,40]{1,0:T(1,128)} %map_hbm.1, s32[4]{0:T(128)} %owner_hbm.1, s32[1,128]{1,0:T(1,128)} %bitcast.9, f32[40,128]{1,0:T(8,128)} %bitcast.8, f32[120,128]{1,0:T(8,128)} %bitcast.7, bf16[1,8,128,128]{3,2,1,0:T(8,128)(2,1)} %lodf_hbm.1, ...), custom_call_target="tpu_custom_call" | custom-call | tf_op jit(solution)/shard_map/dual_step/pallas_call | solution.py:333
  25.4 2.7 %copy.15 = f32[1,8,12,128,128]{4,3,2,1,0:T(8,128)} copy(f32[1,8,12,128,128]{4,3,2,1,0:T(8,128)S(1)} %bitcast.5) | data formatting | bytes 12582912
  28.1 0.6 %copy.16 = f32[1,12,1280]{2,0,1:T(1,128)} copy(f32[1,12,1280]{2,0,1:T(1,128)S(1)} %bitcast.6) | data formatting | bytes 122880
  28.7 0.6 %copy.17 = f32[12,128]{1,0:T(8,128)} copy(f32[12,128]{1,0:T(8,128)S(1)} %get-tuple-element.20) | data formatting | bytes 12288

commit v4 on v3

--- a/solution.py
+++ b/solution.py
@@ -71,7 +71,7 @@
 
 
 def kernel(
-    n_ctg, n_line, outages,
+    n_ctg, n_line, outages, hours,
     map_hbm, owner_hbm, outage_hbm, rating_hbm, own_hbm, lodf_hbm, mult_hbm,
     new_ref, line_ref, grad_ref,
     map_ref, owner_ref, outage_ref, rating_ref,
@@ -80,7 +80,8 @@
     small_sem, mult_sem, lodf_sem, own_sem, flow_ssem, flow_rsem, map_ssem, map_rsem,
     part_ssem, part_rsem, dir_ssem, dir_rsem, grad_ssem, grad_rsem,
 ):
-    slots, hours, tile, _ = mult.shape
+    slots, _, tile, _ = mult.shape
+    groups, span = part.shape[1:3]
     inner = flows.shape[1] // hours
     piece = inner * tile
     me_c = lax.axis_index("ctg")
@@ -91,6 +92,18 @@
 
     def other_l(d):
         return lax.rem(me_l + d, n_line)
+
+    def to_ctg(src, dst, ssem, rsem, d):
+        return pltpu.make_async_remote_copy(
+            src_ref=src, dst_ref=dst, send_sem=ssem, recv_sem=rsem,
+            device_id={"ctg": other_c(d)}, device_id_type=MESH,
+        )
+
+    def to_line(src, dst, ssem, rsem, d):
+        return pltpu.make_async_remote_copy(
+            src_ref=src, dst_ref=dst, send_sem=ssem, recv_sem=rsem,
+            device_id={"line": other_l(d)}, device_id_type=MESH,
+        )
 
     barrier = pltpu.get_barrier_semaphore()
     for d in range(1, n_ctg):
@@ -121,22 +134,17 @@
     own_copy.wait()
     pl.semaphore_wait(barrier, n_ctg - 1 + n_line - 1)
 
+    far = (2, 1, 3) if n_ctg == 4 else tuple(range(1, n_ctg))
     flow_copies = []
-    for d in range(1, n_ctg):
-        copy = pltpu.make_async_remote_copy(
-            src_ref=flows.at[me_c], dst_ref=flows.at[me_c],
-            send_sem=flow_ssem.at[d], recv_sem=flow_rsem.at[d],
-            device_id={"ctg": other_c(d)}, device_id_type=MESH,
-        )
-        copy.start()
-        flow_copies.append(copy)
+    for g in range(groups):
+        rows = flows.at[me_c, pl.ds(g * span * inner, span * inner)]
+        copies = [to_ctg(rows, rows, flow_ssem.at[g, d], flow_rsem.at[g, d], d) for d in far]
+        for copy in copies:
+            copy.start()
+        flow_copies.append(copies)
     map_copies = []
     for d in range(1, n_ctg):
-        copy = pltpu.make_async_remote_copy(
-            src_ref=map_send.at[other_c(d)], dst_ref=map_recv.at[me_c],
-            send_sem=map_ssem.at[d], recv_sem=map_rsem.at[d],
-            device_id={"ctg": other_c(d)}, device_id_type=MESH,
-        )
+        copy = to_ctg(map_send.at[other_c(d)], map_recv.at[me_c], map_ssem.at[d], map_rsem.at[d], d)
         copy.start()
         map_copies.append(copy)
     map_recv[me_c] = map_send[me_c]
@@ -173,150 +181,167 @@
     lax.fori_loop(0, slots, lodf_body, 0)
     acc[...] = jnp.zeros_like(acc)
 
-    def pick(c):
-        value = jnp.concatenate(
-            [flows[c, pl.ds(i, hours, stride=inner), :] for i in range(inner)], axis=1
-        )
-        high = value.astype(jnp.bfloat16)
-        rest = value - high.astype(jnp.float32)
-        middle = rest.astype(jnp.bfloat16)
-        low = (rest - middle.astype(jnp.float32)).astype(jnp.bfloat16)
-        table = onehot[c]
-        total = jnp.dot(high, table, preferred_element_type=jnp.float32)
-        total = total + jnp.dot(middle, table, preferred_element_type=jnp.float32)
-        return total + jnp.dot(low, table, preferred_element_type=jnp.float32)
-
-    def place(c, found):
-        hits = []
+    block_at = []
+    for c in range(n_ctg):
         for i in range(inner):
             block = jnp.int32(-1)
             for q in range(n_ctg):
                 block = jnp.where(owner_ref[c] == q, map_ref[0, q * inner + i], block)
-            hits.append(slot_iota == block)
-        out = []
-        for t in range(hours):
-            rows = found[t]
+            block_at.append(block)
+
+    def pick(c, g):
+        value = jnp.concatenate(
+            [flows[c, pl.ds(g * span * inner + i, span, stride=inner), :] for i in range(inner)], axis=1
+        )
+        high = value.astype(jnp.bfloat16).astype(jnp.float32)
+        rest = value - high
+        middle = rest.astype(jnp.bfloat16).astype(jnp.float32)
+        low = rest - middle
+        parts = jnp.concatenate([high, middle, low, jnp.zeros_like(low)], axis=0).astype(jnp.bfloat16)
+        total = jnp.dot(parts, onehot[c], preferred_element_type=jnp.float32)
+        return total[:span] + total[span : 2 * span] + total[2 * span : 3 * span]
+
+    def gather(g):
+        for copy in flow_copies[g]:
+            copy.wait_recv()
+        picked = pick(0, g)
+        for c in range(1, n_ctg):
+            picked = picked + pick(c, g)
+        part[me_l, g] = picked
+        mine = part.at[me_l, g]
+        copies = [
+            to_line(mine, mine, part_ssem.at[g, d], part_rsem.at[g, d], d) for d in range(1, n_line)
+        ]
+        for copy in copies:
+            copy.start()
+        found = [jnp.zeros((slots, LANES), jnp.float32)] * span
+        for c in range(n_ctg):
             for i in range(inner):
-                row = flows[c, pl.ds(t * inner + i, 1), :]
-                rows = jnp.where(hits[i], jnp.broadcast_to(row, (slots, LANES)), rows)
-            out.append(rows)
-        return out
-
-    order = [me_c]
-    picked = pick(me_c)
-    for d in (1, 3, 2) if n_ctg == 4 else range(1, n_ctg):
-        flow_copies[d - 1].wait_recv()
-        order.append(lax.rem(me_c + n_ctg - d, n_ctg))
-        picked = picked + pick(order[-1])
-    part[me_l] = picked
-    part_copies = []
-    for d in range(1, n_line):
-        copy = pltpu.make_async_remote_copy(
-            src_ref=part.at[me_l], dst_ref=part.at[me_l],
-            send_sem=part_ssem.at[d], recv_sem=part_rsem.at[d],
-            device_id={"line": other_l(d)}, device_id_type=MESH,
-        )
+                hit = slot_iota == block_at[c * inner + i]
+                for t in range(span):
+                    row = flows[c, pl.ds((g * span + t) * inner + i, 1), :]
+                    found[t] = jnp.where(hit, jnp.broadcast_to(row, (slots, LANES)), found[t])
+        for t in range(span):
+            slot_flow[g * span + t] = found[t]
+        return copies
+
+    def update(g, part_copies):
+        for copy in part_copies:
+            copy.wait_recv()
+        outage = part[0, g]
+        for j in range(1, n_line):
+            outage = outage + part[j, g]
+        turned = jnp.concatenate([outage, jnp.zeros((ROWS - span, LANES), jnp.float32)], axis=0).T
+        for t in range(span):
+            spread[t] = jnp.broadcast_to(turned[:, t : t + 1], (tile, LANES))
+        first = g * span
+
+        def pair_body(p, carry):
+            pair = [2 * p, 2 * p + 1]
+            if g == 0:
+                for s in pair:
+                    pltpu.make_async_copy(mult_hbm.at[0, s], mult.at[s], mult_sem.at[s]).wait()
+
+            def lines(ref, s):
+                return jnp.broadcast_to(ref[pl.ds(s, 1), :], (ROWS, LANES))
+
+            half = [lines(slot_half, s) for s in pair]
+            bar = [lines(slot_bar, s) for s in pair]
+            base = [[lines(slot_flow.at[first + t], s) for t in range(span)] for s in pair]
+
+            def row_body(k, sums):
+                row = pl.multiple_of(k * ROWS, ROWS)
+                rows = pl.ds(row, ROWS)
+                factor = [lodf[s, rows, :] for s in pair]
+                out = [None] * (2 * span)
+                for t in range(span):
+                    flow = spread[t, rows, :]
+                    total = acc[first + t, rows, :]
+                    for e, s in enumerate(pair):
+                        post = base[e][t] + factor[e] * flow
+                        scaled = post * half[e]
+                        updated = jnp.maximum(
+                            mult[s, first + t, rows, :] + (post * scaled - bar[e]), 0.0
+                        )
+                        new_ref[s, first + t, rows, :] = updated
+                        weight = updated * scaled
+                        total = total + factor[e] * weight
+                        out[e * span + t] = sums[e * span + t] + weight
+                    acc[first + t, rows, :] = total
+                return tuple(out)
+
+            zero = jnp.zeros((ROWS, LANES), jnp.float32)
+            sums = lax.fori_loop(0, tile // ROWS, row_body, (zero,) * (2 * span), unroll=2)
+            for e, s in enumerate(pair):
+                for t in range(span):
+                    direct[me_c, g, pl.ds(s * span + t, 1), :] = jnp.sum(
+                        sums[e * span + t], axis=0, keepdims=True
+                    )
+            return carry
+
+        lax.fori_loop(0, slots // 2, pair_body, 0)
+        mine = direct.at[me_c, g]
+        copies = [to_ctg(mine, mine, dir_ssem.at[g, d], dir_rsem.at[g, d], d) for d in far]
+        for copy in copies:
+            copy.start()
+        columns = lax.broadcasted_iota(jnp.int32, (tile, LANES), 1)
+        packed = jnp.zeros((tile, LANES), jnp.float32)
+        for t in range(span):
+            packed = jnp.where(columns == t, jnp.sum(acc[first + t], axis=1, keepdims=True), packed)
+        grad[me_l, g] = packed.T[:span]
+        return copies
+
+    def combine(g, direct_copies):
+        for copy in direct_copies:
+            copy.wait_recv()
+        for t in range(span):
+            total = jnp.zeros((inner, LANES), jnp.float32)
+            for c in range(n_ctg):
+                which = map_recv[c]
+                for s in range(slots):
+                    row = direct[c, g, pl.ds(s * span + t, 1), :]
+                    total = total + jnp.where(which == s, jnp.broadcast_to(row, (inner, LANES)), 0.0)
+            line_ref[pl.ds((g * span + t) * inner, inner), :] = total * (1.0 / dual_step / outages)
+
+    part_copies, direct_copies = [], []
+    for g in range(groups):
+        part_copies.append(gather(g))
+        if g >= 1:
+            direct_copies.append(update(g - 1, part_copies[g - 1]))
+    direct_copies.append(update(groups - 1, part_copies[groups - 1]))
+
+    mine = grad.at[me_l]
+    grad_copies = [to_line(mine, mine, grad_ssem.at[d], grad_rsem.at[d], d) for d in range(1, n_line)]
+    for copy in grad_copies:
         copy.start()
-        part_copies.append(copy)
-
-    found = [jnp.zeros((slots, LANES), jnp.float32)] * hours
-    for c in range(n_ctg):
-        found = place(c, found)
-    for t in range(hours):
-        slot_flow[t] = found[t]
-
-    for copy in part_copies:
-        copy.wait_recv()
-    outage = part[0]
-    for j in range(1, n_line):
-        outage = outage + part[j]
-    turned = jnp.concatenate([outage, jnp.zeros((16 - hours, LANES), jnp.float32)], axis=0).T
-    for t in range(hours):
-        spread[t] = jnp.broadcast_to(turned[:, t : t + 1], (tile, LANES))
-
-    def direct_copy(s, d):
-        return pltpu.make_async_remote_copy(
-            src_ref=direct.at[me_c, s], dst_ref=direct.at[me_c, s],
-            send_sem=dir_ssem.at[s, d], recv_sem=dir_rsem.at[s, d],
-            device_id={"ctg": other_c(d)}, device_id_type=MESH,
-        )
-
-    def slot_body(s, carry):
-        pltpu.make_async_copy(mult_hbm.at[0, s], mult.at[s], mult_sem.at[s]).wait()
-        half = jnp.broadcast_to(slot_half[pl.ds(s, 1), :], (ROWS, LANES))
-        bar = jnp.broadcast_to(slot_bar[pl.ds(s, 1), :], (ROWS, LANES))
-        base = [
-            jnp.broadcast_to(slot_flow[t, pl.ds(s, 1), :], (ROWS, LANES)) for t in range(hours)
-        ]
-
-        def row_body(k, sums):
-            row = pl.multiple_of(k * ROWS, ROWS)
-            factor = lodf[s, pl.ds(row, ROWS), :]
-            out = []
-            for t in range(hours):
-                post = base[t] + factor * spread[t, pl.ds(row, ROWS), :]
-                scaled = post * half
-                updated = jnp.maximum(mult[s, t, pl.ds(row, ROWS), :] + (post * scaled - bar), 0.0)
-                new_ref[s, t, pl.ds(row, ROWS), :] = updated
-                weight = updated * scaled
-                acc[t, pl.ds(row, ROWS), :] += factor * weight
-                out.append(sums[t] + weight)
-            return tuple(out)
-
-        zero = jnp.zeros((ROWS, LANES), jnp.float32)
-        sums = lax.fori_loop(0, tile // ROWS, row_body, (zero,) * hours)
-        for t in range(hours):
-            direct[me_c, s, pl.ds(t, 1), :] = jnp.sum(sums[t], axis=0, keepdims=True)
-        for d in range(1, n_ctg):
-            direct_copy(s, d).start()
-        return carry
-
-    lax.fori_loop(0, slots, slot_body, 0)
-
-    columns = lax.broadcasted_iota(jnp.int32, (tile, LANES), 1)
-    packed = jnp.zeros((tile, LANES), jnp.float32)
-    for t in range(hours):
-        packed = jnp.where(columns == t, jnp.sum(acc[t], axis=1, keepdims=True), packed)
-    grad[me_l] = packed.T[:hours]
-    grad_copies = []
-    for d in range(1, n_line):
-        copy = pltpu.make_async_remote_copy(
-            src_ref=grad.at[me_l], dst_ref=grad.at[me_l],
-            send_sem=grad_ssem.at[d], recv_sem=grad_rsem.at[d],
-            device_id={"line": other_l(d)}, device_id_type=MESH,
-        )
-        copy.start()
-        grad_copies.append(copy)
 
     for copy in map_copies:
         copy.wait_recv()
-
-    def direct_wait(s, carry):
-        for d in range(1, n_ctg):
-            direct_copy(s, d).wait()
-        return carry
-
-    lax.fori_loop(0, slots, direct_wait, 0)
-
-    for i in range(inner):
-        total = jnp.zeros((hours, LANES), jnp.float32)
-        for c in range(n_ctg):
-            which = jnp.broadcast_to(map_recv[c, pl.ds(i, 1), :], (hours, LANES))
-            found = jnp.zeros((hours, LANES), jnp.float32)
-            for s in range(slots):
-                found = jnp.where(which == s, direct[c, s], found)
-            total = total + found
-        line_ref[pl.ds(i, hours, stride=inner), :] = total * (1.0 / dual_step / outages)
+    for g in range(groups):
+        combine(g, direct_copies[g])
 
     for copy in grad_copies:
         copy.wait_recv()
-    total = grad[0]
-    for j in range(1, n_line):
-        total = total + grad[j]
-    grad_ref[...] = total * (outage_scale / dual_step)
-
-    for copy in flow_copies + map_copies + part_copies + grad_copies:
-        copy.wait_send()
+    for g in range(groups):
+        total = grad[0, g]
+        for j in range(1, n_line):
+            total = total + grad[j, g]
+        grad_ref[pl.ds(g * span, span), :] = total * (outage_scale / dual_step)
+
+    for copies in flow_copies + part_copies + direct_copies + [map_copies, grad_copies]:
+        for copy in copies:
+            copy.wait_send()
+
+
+def write_out(new_vmem, line_vmem, grad_vmem, new_hbm, line_hbm, grad_hbm, sems):
+    slots = new_vmem.shape[0]
+    copies = [pltpu.make_async_copy(new_vmem.at[s], new_hbm.at[s], sems.at[s]) for s in range(slots)]
+    copies.append(pltpu.make_async_copy(line_vmem, line_hbm, sems.at[slots]))
+    copies.append(pltpu.make_async_copy(grad_vmem, grad_hbm, sems.at[slots + 1]))
+    for copy in copies:
+        copy.start()
+    for copy in copies:
+        copy.wait()
 
 
 def per_device_fused(owned_flow, ratings, lodf_tiles, tile_map, outage_line, block_owner, multipliers):
@@ -326,17 +351,21 @@
     _, slots, tile, _ = lodf_tiles.shape
     inner = piece // tile
     outages = outage_line.shape[0] * n_ctg
+    span = 4
+    groups = hours // span
     f32, bf16, i32 = jnp.float32, jnp.bfloat16, jnp.int32
     dma = pltpu.SemaphoreType.DMA
     vmem = pl.BlockSpec(memory_space=pltpu.VMEM)
     hbm = pl.BlockSpec(memory_space=pltpu.HBM)
-    updated, line_gradient, outage_gradient = pl.pallas_call(
-        functools.partial(kernel, n_ctg, n_line, outages),
-        out_shape=(
-            jax.ShapeDtypeStruct((slots, hours, tile, tile), f32),
-            jax.ShapeDtypeStruct((hours * inner, tile), f32),
-            jax.ShapeDtypeStruct((hours, tile), f32),
-        ),
+    anywhere = pl.BlockSpec(memory_space=pl.ANY)
+    shapes = (
+        jax.ShapeDtypeStruct((slots, hours, tile, tile), f32),
+        jax.ShapeDtypeStruct((hours * inner, tile), f32),
+        jax.ShapeDtypeStruct((hours, tile), f32),
+    )
+    results = pl.pallas_call(
+        functools.partial(kernel, n_ctg, n_line, outages, hours),
+        out_shape=shapes,
         in_specs=[hbm] * 7,
         out_specs=(vmem, vmem, vmem),
         scratch_shapes=[
@@ -352,17 +381,17 @@
             pltpu.VMEM((hours, slots, tile), f32),
             pltpu.VMEM((slots, tile), f32),
             pltpu.VMEM((slots, tile), f32),
+            pltpu.VMEM((span, tile, tile), f32),
             pltpu.VMEM((hours, tile, tile), f32),
-            pltpu.VMEM((hours, tile, tile), f32),
-            pltpu.VMEM((n_ctg, slots, hours, tile), f32),
+            pltpu.VMEM((n_ctg, groups, slots * span, tile), f32),
             pltpu.VMEM((n_ctg, inner, tile), i32),
             pltpu.VMEM((n_ctg, inner, tile), i32),
-            pltpu.VMEM((n_line, hours, tile), f32),
-            pltpu.VMEM((n_line, hours, tile), f32),
+            pltpu.VMEM((n_line, groups, span, tile), f32),
+            pltpu.VMEM((n_line, groups, span, tile), f32),
             dma((4,)), dma((slots,)), dma, dma,
-            dma((n_ctg,)), dma((n_ctg,)), dma((n_ctg,)), dma((n_ctg,)),
-            dma((n_line,)), dma((n_line,)),
-            dma((slots, n_ctg)), dma((slots, n_ctg)),
+            dma((groups, n_ctg)), dma((groups, n_ctg)), dma((n_ctg,)), dma((n_ctg,)),
+            dma((groups, n_line)), dma((groups, n_line)),
+            dma((groups, n_ctg)), dma((groups, n_ctg)),
             dma((n_line,)), dma((n_line,)),
         ],
         compiler_params=pltpu.CompilerParams(
@@ -379,6 +408,14 @@
             )
         )
     )
+    updated, line_gradient, outage_gradient = pl.pallas_call(
+        write_out,
+        out_shape=shapes,
+        in_specs=[anywhere] * 3,
+        out_specs=(anywhere,) * 3,
+        scratch_shapes=[dma((slots + 2,))],
+        name="write_out",
+    )(*results)
     return updated[None], line_gradient.reshape(1, hours, piece), outage_gradient
 
 
@@ -387,7 +424,8 @@
     tile = lodf_tiles.shape[-1]
     whole = (
         tile == LANES
-        and owned_flow.shape[1] <= 16
+        and owned_flow.shape[1] % 4 == 0
+        and lodf_tiles.shape[1] == 8
         and owned_flow.shape[2] % tile == 0
         and outage_line.shape[0] == tile
         and lodf_tiles.shape[0] == 1

time: 29.5 us -> 222 us (7.53)
  Pallas kernels: 24.8 us -> 217 us
    pallas_call x1 -> x2, Pallas kernels: 24.8 us -> 217 us  [the longest x1 194 us: per_device_fused(): pl.pallas_call(write_out, out_shape=shapes, in_specs=[anywhere] * 3, out_...]
where the time goes in v4:
time: 222 us
  Pallas kernels  217 us (98%)
  local copies, waits for them, and re-layouts  3.87 us (2%)
    pallas_call x1, Pallas kernels, per_device_fused(): pl.pallas_call(write_out, out_shape=shapes, in_specs=[anywhere] * 3, out_...  194 us
    pallas_call x1, Pallas kernels, per_device_fused(): pl.pallas_call(functools.partial(kernel, n_ctg, n_line, outages, hours),...  23.4 us

profile of v4, /device:TPU:0, one launch (start us, length us, event | category | flops | bytes accessed | tf_op | source)
XLA Modules:
  0.0 221.7 jit_solution(7029984341295356812)
XLA Ops:
  0.6 23.4 %dual_step.1 = (f32[8,12,128,128]{3,2,1,0:T(8,128)S(1)}, f32[120,128]{1,0:T(8,128)S(1)}, f32[12,128]{1,0:T(8,128)S(1)}) custom-call(s32[1,40]{1,0:T(1,128)} %map_hbm.1, s32[4]{0:T(128)} %owner_hbm.1, s32[1,128]{1,0:T(1,128)} %bitcast.7, f32[40,128]{1,0:T(8,128)} %bitcast.6, f32[120,128]{1,0:T(8,128)} %bitcast.5, bf16[1,8,128,128]{3,2,1,0:T(8,128)(2,1)} %lodf_hbm.1, ...), custom_call_target="tpu_custom_call" | custom-call | tf_op jit(solution)/shard_map/dual_step/pallas_call | solution.py:366
  24.0 0.0 copy-start
  24.0 2.6 %copy-done = f32[8,12,128,128]{3,2,1,0:T(8,128)} copy-done((f32[8,12,128,128]{3,2,1,0:T(8,128)}, f32[8,12,128,128]{3,2,1,0:T(8,128)S(1)}, u32[]{:S(2)}) %copy-start) | copy-done | bytes 6291480
  26.7 0.0 copy-start.1
  26.7 0.6 copy-done.1
  27.3 0.0 copy-start.2
  27.3 0.6 copy-done.2
  27.9 193.8 %write_out.1 = (f32[8,12,128,128]{3,2,1,0:T(8,128)}, f32[120,128]{1,0:T(8,128)}, f32[12,128]{1,0:T(8,128)}) custom-call(f32[8,12,128,128]{3,2,1,0:T(8,128)} %copy-done, f32[120,128]{1,0:T(8,128)} %copy-done.1, f32[12,128]{1,0:T(8,128)} %copy-done.2), custom_call_target="tpu_custom_call" | custom-call | tf_op jit(solution)/shard_map/write_out/pallas_call | solution.py:411
Async XLA Ops:
  24.0 2.7 %copy-start = (f32[8,12,128,128]{3,2,1,0:T(8,128)}, f32[8,12,128,128]{3,2,1,0:T(8,128)S(1)}, u32[]{:S(2)}) copy-start(f32[8,12,128,128]{3,2,1,0:T(8,128)S(1)} %get-tuple-element.9.new_vmem) | copy-start | bytes 18874372
  26.7 0.6 copy-start.1
  27.3 0.6 copy-start.2

commit v5 on v4

--- a/solution.py
+++ b/solution.py
@@ -357,7 +357,6 @@
     dma = pltpu.SemaphoreType.DMA
     vmem = pl.BlockSpec(memory_space=pltpu.VMEM)
     hbm = pl.BlockSpec(memory_space=pltpu.HBM)
-    anywhere = pl.BlockSpec(memory_space=pl.ANY)
     shapes = (
         jax.ShapeDtypeStruct((slots, hours, tile, tile), f32),
         jax.ShapeDtypeStruct((hours * inner, tile), f32),
@@ -411,11 +410,12 @@
     updated, line_gradient, outage_gradient = pl.pallas_call(
         write_out,
         out_shape=shapes,
-        in_specs=[anywhere] * 3,
-        out_specs=(anywhere,) * 3,
+        in_specs=[vmem] * 3,
+        out_specs=(hbm,) * 3,
         scratch_shapes=[dma((slots + 2,))],
+        compiler_params=pltpu.CompilerParams(vmem_limit_bytes=40 * 1024 * 1024),
         name="write_out",
-    )(*results)
+    )(*(pltpu.with_memory_space_constraint(x, pltpu.VMEM) for x in results))
     return updated[None], line_gradient.reshape(1, hours, piece), outage_gradient
 
 

time: 222 us -> 26.9 us (0.12)
  Pallas kernels: 217 us -> 26.1 us
  local copies, waits for them, and re-layouts: 3.87 us -> 0 us
    pallas_call x1, Pallas kernels: 194 us -> 2.76 us  [per_device_fused(): pl.pallas_call(write_out, out_shape=shapes, in_specs=[vmem] * 3, out_spec...]
    unnamed x6 -> x0, local copies, waits for them, and re-layouts: 3.87 us -> none
where the time goes in v5:
time: 26.9 us; the launch traced here: 26.8 us
  Pallas kernels  26.1 us (97%)
  between operations  0.64 us (2%)
    pallas_call x1, Pallas kernels, per_device_fused(): pl.pallas_call(functools.partial(kernel, n_ctg, n_line, outages, hours),...  23.4 us
    pallas_call x1, Pallas kernels, per_device_fused(): pl.pallas_call(write_out, out_shape=shapes, in_specs=[vmem] * 3, out_spec...  2.76 us

profile of v5, /device:TPU:0, one launch (start us, length us, event | category | flops | bytes accessed | tf_op | source)
XLA Modules:
  0.0 26.8 jit_solution(3790514647633791586)
XLA Ops:
  0.6 23.4 %dual_step.1 = (f32[8,12,128,128]{3,2,1,0:T(8,128)S(1)}, f32[120,128]{1,0:T(8,128)S(1)}, f32[12,128]{1,0:T(8,128)S(1)}) custom-call(s32[1,40]{1,0:T(1,128)} %map_hbm.1, s32[4]{0:T(128)} %owner_hbm.1, s32[1,128]{1,0:T(1,128)} %bitcast.7, f32[40,128]{1,0:T(8,128)} %bitcast.6, f32[120,128]{1,0:T(8,128)} %bitcast.5, bf16[1,8,128,128]{3,2,1,0:T(8,128)(2,1)} %lodf_hbm.1, ...), custom_call_target="tpu_custom_call" | custom-call | tf_op jit(solution)/shard_map/dual_step/pallas_call | solution.py:365
  24.0 2.8 %write_out.1 = (f32[8,12,128,128]{3,2,1,0:T(8,128)}, f32[120,128]{1,0:T(8,128)}, f32[12,128]{1,0:T(8,128)}) custom-call(f32[8,12,128,128]{3,2,1,0:T(8,128)S(1)} %get-tuple-element.9.new_vmem, f32[120,128]{1,0:T(8,128)S(1)} %get-tuple-element.10.line_vmem, f32[12,128]{1,0:T(8,128)S(1)} %get-tuple-element.11.grad_vmem), custom_call_target="tpu_custom_call" | custom-call | tf_op jit(solution)/shard_map/write_out/pallas_call | solution.py:410

commit v6 on v5

--- a/solution.py
+++ b/solution.py
@@ -74,14 +74,14 @@
     n_ctg, n_line, outages, hours,
     map_hbm, owner_hbm, outage_hbm, rating_hbm, own_hbm, lodf_hbm, mult_hbm,
     new_ref, line_ref, grad_ref,
-    map_ref, owner_ref, outage_ref, rating_ref,
+    map_ref, owner_ref, ids, rating_ref,
     mult, lodf16, lodf, flows, onehot, slot_flow, slot_half, slot_bar, spread, acc, direct,
-    map_send, map_recv, part, grad,
-    small_sem, mult_sem, lodf_sem, own_sem, flow_ssem, flow_rsem, map_ssem, map_rsem,
+    map_send, map_recv, outbox, part, grad,
+    small_sem, mult_sem, lodf_sem, own_sem, id_ssem, id_rsem, flow_ssem, flow_rsem, map_ssem, map_rsem,
     part_ssem, part_rsem, dir_ssem, dir_rsem, grad_ssem, grad_rsem,
 ):
     slots, _, tile, _ = mult.shape
-    groups, span = part.shape[1:3]
+    groups, span = grad.shape[1:3]
     inner = flows.shape[1] // hours
     piece = inner * tile
     me_c = lax.axis_index("ctg")
@@ -106,17 +106,18 @@
         )
 
     barrier = pltpu.get_barrier_semaphore()
-    for d in range(1, n_ctg):
-        pl.semaphore_signal(barrier, inc=1, device_id={"ctg": other_c(d)}, device_id_type=MESH)
-    for d in range(1, n_line):
-        pl.semaphore_signal(barrier, inc=1, device_id={"line": other_l(d)}, device_id_type=MESH)
+    others = [(dc, dl) for dc in range(n_ctg) for dl in range(n_line) if (dc, dl) != (0, 0)]
+    for dc, dl in others:
+        pl.semaphore_signal(
+            barrier, inc=1, device_id={"ctg": other_c(dc), "line": other_l(dl)}, device_id_type=MESH
+        )
 
     own_copy = pltpu.make_async_copy(own_hbm, flows.at[me_c], own_sem)
     own_copy.start()
     small_copies = [
         pltpu.make_async_copy(src, dst, small_sem.at[i])
         for i, (src, dst) in enumerate(
-            ((map_hbm, map_ref), (owner_hbm, owner_ref), (outage_hbm, outage_ref), (rating_hbm, rating_ref))
+            ((map_hbm, map_ref), (owner_hbm, owner_ref), (outage_hbm, ids.at[me_c]), (rating_hbm, rating_ref))
         )
     ]
     for copy in small_copies:
@@ -126,13 +127,14 @@
     for s in range(slots):
         pltpu.make_async_copy(mult_hbm.at[0, s], mult.at[s], mult_sem.at[s]).start()
 
-    for copy in small_copies:
-        copy.wait()
-    for q in range(n_ctg):
-        for i in range(inner):
-            map_send[q, pl.ds(i, 1), :] = jnp.full((1, LANES), map_ref[0, q * inner + i], jnp.int32)
     own_copy.wait()
-    pl.semaphore_wait(barrier, n_ctg - 1 + n_line - 1)
+    small_copies[2].wait()
+    pl.semaphore_wait(barrier, len(others))
+
+    mine = ids.at[me_c]
+    id_copies = [to_ctg(mine, mine, id_ssem.at[d], id_rsem.at[d], d) for d in range(1, n_ctg)]
+    for copy in id_copies:
+        copy.start()
 
     far = (2, 1, 3) if n_ctg == 4 else tuple(range(1, n_ctg))
     flow_copies = []
@@ -142,6 +144,11 @@
         for copy in copies:
             copy.start()
         flow_copies.append(copies)
+    for i in (0, 1, 3):
+        small_copies[i].wait()
+    for q in range(n_ctg):
+        for i in range(inner):
+            map_send[q, pl.ds(i, 1), :] = jnp.full((1, LANES), map_ref[0, q * inner + i], jnp.int32)
     map_copies = []
     for d in range(1, n_ctg):
         copy = to_ctg(map_send.at[other_c(d)], map_recv.at[me_c], map_ssem.at[d], map_rsem.at[d], d)
@@ -149,18 +156,43 @@
         map_copies.append(copy)
     map_recv[me_c] = map_send[me_c]
 
+    for copy in id_copies:
+        copy.wait_recv()
     rows_iota = lax.broadcasted_iota(jnp.int32, (tile, LANES), 0)
+    base = (me_l * n_ctg + owner_ref[me_c]) * piece
     for c in range(n_ctg):
-        base = (me_l * n_ctg + owner_ref[c]) * piece
-        wanted = jnp.broadcast_to(outage_ref[...] - base, (tile, LANES))
+        wanted = jnp.broadcast_to(ids[c] - base, (tile, LANES))
 
         def hot_body(b, carry, c=c, wanted=wanted):
             row = pl.multiple_of(b * tile, tile)
             hit = (rows_iota + row) == wanted
-            onehot[c, pl.ds(row, tile), :] = jnp.where(hit, 1.0, 0.0).astype(jnp.bfloat16)
+            onehot[pl.ds(row, tile), c * tile : (c + 1) * tile] = jnp.where(hit, 1.0, 0.0).astype(jnp.bfloat16)
             return carry
 
         lax.fori_loop(0, inner, hot_body, 0)
+    value = jnp.concatenate(
+        [flows[me_c, pl.ds(i, hours, stride=inner), :] for i in range(inner)], axis=1
+    )
+    value = jnp.concatenate([value, jnp.zeros((16 - hours, piece), jnp.float32)], axis=0)
+    high = value.astype(jnp.bfloat16).astype(jnp.float32)
+    rest = value - high
+    middle = rest.astype(jnp.bfloat16).astype(jnp.float32)
+    low = rest - middle
+    parts = jnp.concatenate([high, middle, low], axis=0).astype(jnp.bfloat16)
+    picked = jnp.dot(parts, onehot[...], preferred_element_type=jnp.float32)
+    picked = picked[:16] + picked[16:32] + picked[32:]
+    for c in range(n_ctg):
+        outbox[c] = picked[:hours, c * tile : (c + 1) * tile]
+    part_copies = []
+    for dc, dl in others:
+        copy = pltpu.make_async_remote_copy(
+            src_ref=outbox.at[other_c(dc)], dst_ref=part.at[me_c, me_l],
+            send_sem=part_ssem.at[dc, dl], recv_sem=part_rsem.at[dc, dl],
+            device_id={"ctg": other_c(dc), "line": other_l(dl)}, device_id_type=MESH,
+        )
+        copy.start()
+        part_copies.append(copy)
+    part[me_c, me_l] = outbox[me_c]
 
     slot_iota = lax.broadcasted_iota(jnp.int32, (slots, LANES), 0)
     rating = jnp.ones((slots, LANES), jnp.float32)
@@ -189,31 +221,9 @@
                 block = jnp.where(owner_ref[c] == q, map_ref[0, q * inner + i], block)
             block_at.append(block)
 
-    def pick(c, g):
-        value = jnp.concatenate(
-            [flows[c, pl.ds(g * span * inner + i, span, stride=inner), :] for i in range(inner)], axis=1
-        )
-        high = value.astype(jnp.bfloat16).astype(jnp.float32)
-        rest = value - high
-        middle = rest.astype(jnp.bfloat16).astype(jnp.float32)
-        low = rest - middle
-        parts = jnp.concatenate([high, middle, low, jnp.zeros_like(low)], axis=0).astype(jnp.bfloat16)
-        total = jnp.dot(parts, onehot[c], preferred_element_type=jnp.float32)
-        return total[:span] + total[span : 2 * span] + total[2 * span : 3 * span]
-
     def gather(g):
         for copy in flow_copies[g]:
             copy.wait_recv()
-        picked = pick(0, g)
-        for c in range(1, n_ctg):
-            picked = picked + pick(c, g)
-        part[me_l, g] = picked
-        mine = part.at[me_l, g]
-        copies = [
-            to_line(mine, mine, part_ssem.at[g, d], part_rsem.at[g, d], d) for d in range(1, n_line)
-        ]
-        for copy in copies:
-            copy.start()
         found = [jnp.zeros((slots, LANES), jnp.float32)] * span
         for c in range(n_ctg):
             for i in range(inner):
@@ -223,17 +233,8 @@
                     found[t] = jnp.where(hit, jnp.broadcast_to(row, (slots, LANES)), found[t])
         for t in range(span):
             slot_flow[g * span + t] = found[t]
-        return copies
-
-    def update(g, part_copies):
-        for copy in part_copies:
-            copy.wait_recv()
-        outage = part[0, g]
-        for j in range(1, n_line):
-            outage = outage + part[j, g]
-        turned = jnp.concatenate([outage, jnp.zeros((ROWS - span, LANES), jnp.float32)], axis=0).T
-        for t in range(span):
-            spread[t] = jnp.broadcast_to(turned[:, t : t + 1], (tile, LANES))
+
+    def update(g):
         first = g * span
 
         def pair_body(p, carry):
@@ -255,7 +256,7 @@
                 factor = [lodf[s, rows, :] for s in pair]
                 out = [None] * (2 * span)
                 for t in range(span):
-                    flow = spread[t, rows, :]
+                    flow = spread[first + t, rows, :]
                     total = acc[first + t, rows, :]
                     for e, s in enumerate(pair):
                         post = base[e][t] + factor[e] * flow
@@ -303,12 +304,20 @@
                     total = total + jnp.where(which == s, jnp.broadcast_to(row, (inner, LANES)), 0.0)
             line_ref[pl.ds((g * span + t) * inner, inner), :] = total * (1.0 / dual_step / outages)
 
-    part_copies, direct_copies = [], []
+    for copy in part_copies:
+        copy.wait_recv()
+    outage = jnp.zeros((hours, LANES), jnp.float32)
+    for c in range(n_ctg):
+        for j in range(n_line):
+            outage = outage + part[c, j]
+    turned = jnp.concatenate([outage, jnp.zeros((16 - hours, LANES), jnp.float32)], axis=0).T
+    for t in range(hours):
+        spread[t] = jnp.broadcast_to(turned[:, t : t + 1], (tile, LANES))
+
+    direct_copies = []
     for g in range(groups):
-        part_copies.append(gather(g))
-        if g >= 1:
-            direct_copies.append(update(g - 1, part_copies[g - 1]))
-    direct_copies.append(update(groups - 1, part_copies[groups - 1]))
+        gather(g)
+        direct_copies.append(update(g))
 
     mine = grad.at[me_l]
     grad_copies = [to_line(mine, mine, grad_ssem.at[d], grad_rsem.at[d], d) for d in range(1, n_line)]
@@ -328,7 +337,7 @@
             total = total + grad[j, g]
         grad_ref[pl.ds(g * span, span), :] = total * (outage_scale / dual_step)
 
-    for copies in flow_copies + part_copies + direct_copies + [map_copies, grad_copies]:
+    for copies in flow_copies + direct_copies + [id_copies, map_copies, part_copies, grad_copies]:
         for copy in copies:
             copy.wait_send()
 
@@ -370,26 +379,28 @@
         scratch_shapes=[
             pltpu.SMEM(tile_map.shape, i32),
             pltpu.SMEM(block_owner.shape, i32),
-            pltpu.VMEM((1, tile), i32),
+            pltpu.VMEM((n_ctg, 1, tile), i32),
             pltpu.VMEM((n_ctg * inner, tile), f32),
             pltpu.VMEM((slots, hours, tile, tile), f32),
             pltpu.VMEM((slots, tile, tile), bf16),
             pltpu.VMEM((slots, tile, tile), f32),
             pltpu.VMEM((n_ctg, hours * inner, tile), f32),
-            pltpu.VMEM((n_ctg, piece, tile), bf16),
+            pltpu.VMEM((piece, n_ctg * tile), bf16),
             pltpu.VMEM((hours, slots, tile), f32),
             pltpu.VMEM((slots, tile), f32),
             pltpu.VMEM((slots, tile), f32),
-            pltpu.VMEM((span, tile, tile), f32),
+            pltpu.VMEM((hours, tile, tile), f32),
             pltpu.VMEM((hours, tile, tile), f32),
             pltpu.VMEM((n_ctg, groups, slots * span, tile), f32),
             pltpu.VMEM((n_ctg, inner, tile), i32),
             pltpu.VMEM((n_ctg, inner, tile), i32),
-            pltpu.VMEM((n_line, groups, span, tile), f32),
+            pltpu.VMEM((n_ctg, hours, tile), f32),
+            pltpu.VMEM((n_ctg, n_line, hours, tile), f32),
             pltpu.VMEM((n_line, groups, span, tile), f32),
             dma((4,)), dma((slots,)), dma, dma,
+            dma((n_ctg,)), dma((n_ctg,)),
             dma((groups, n_ctg)), dma((groups, n_ctg)), dma((n_ctg,)), dma((n_ctg,)),
-            dma((groups, n_line)), dma((groups, n_line)),
+            dma((n_ctg, n_line)), dma((n_ctg, n_line)),
             dma((groups, n_ctg)), dma((groups, n_ctg)),
             dma((n_line,)), dma((n_line,)),
         ],
@@ -425,6 +436,7 @@
     whole = (
         tile == LANES
         and owned_flow.shape[1] % 4 == 0
+        and owned_flow.shape[1] <= 12
         and lodf_tiles.shape[1] == 8
         and owned_flow.shape[2] % tile == 0
         and outage_line.shape[0] == tile

time: 26.9 us -> 28.7 us (1.067)
  Pallas kernels: 26.1 us -> 27.9 us
    pallas_call x1, Pallas kernels: 23.4 us -> 25.1 us  [per_device_fused(): pl.pallas_call(functools.partial(kernel, n_ctg, n_line, outages, hours),...]
where the time goes in v6:
time: 28.7 us; the launch traced here: 28.5 us
  Pallas kernels  27.9 us (97%)
  between operations  0.64 us (2%)
    pallas_call x1, Pallas kernels, per_device_fused(): pl.pallas_call(functools.partial(kernel, n_ctg, n_line, outages, hours),...  25.1 us
    pallas_call x1, Pallas kernels, per_device_fused(): pl.pallas_call(write_out, out_shape=shapes, in_specs=[vmem] * 3, out_spec...  2.76 us

profile of v6, /device:TPU:0, one launch (start us, length us, event | category | flops | bytes accessed | tf_op | source)
XLA Modules:
  0.0 28.5 jit_solution(431234083982890478)
XLA Ops:
  0.6 25.1 %dual_step.1 = (f32[8,12,128,128]{3,2,1,0:T(8,128)S(1)}, f32[120,128]{1,0:T(8,128)S(1)}, f32[12,128]{1,0:T(8,128)S(1)}) custom-call(s32[1,40]{1,0:T(1,128)} %map_hbm.1, s32[4]{0:T(128)} %owner_hbm.1, s32[1,128]{1,0:T(1,128)} %bitcast.7, f32[40,128]{1,0:T(8,128)} %bitcast.6, f32[120,128]{1,0:T(8,128)} %bitcast.5, bf16[1,8,128,128]{3,2,1,0:T(8,128)(2,1)} %lodf_hbm.1, ...), custom_call_target="tpu_custom_call" | custom-call | tf_op jit(solution)/shard_map/dual_step/pallas_call | solution.py:374
  25.7 2.8 %write_out.1 = (f32[8,12,128,128]{3,2,1,0:T(8,128)}, f32[120,128]{1,0:T(8,128)}, f32[12,128]{1,0:T(8,128)}) custom-call(f32[8,12,128,128]{3,2,1,0:T(8,128)S(1)} %get-tuple-element.9.new_vmem, f32[120,128]{1,0:T(8,128)S(1)} %get-tuple-element.10.line_vmem, f32[12,128]{1,0:T(8,128)S(1)} %get-tuple-element.11.grad_vmem), custom_call_target="tpu_custom_call" | custom-call | tf_op jit(solution)/shard_map/write_out/pallas_call | solution.py:421

commit v7 on v5

--- a/solution.py
+++ b/solution.py
@@ -126,11 +126,6 @@
     for s in range(slots):
         pltpu.make_async_copy(mult_hbm.at[0, s], mult.at[s], mult_sem.at[s]).start()
 
-    for copy in small_copies:
-        copy.wait()
-    for q in range(n_ctg):
-        for i in range(inner):
-            map_send[q, pl.ds(i, 1), :] = jnp.full((1, LANES), map_ref[0, q * inner + i], jnp.int32)
     own_copy.wait()
     pl.semaphore_wait(barrier, n_ctg - 1 + n_line - 1)
 
@@ -142,6 +137,11 @@
         for copy in copies:
             copy.start()
         flow_copies.append(copies)
+    for copy in small_copies:
+        copy.wait()
+    for q in range(n_ctg):
+        for i in range(inner):
+            map_send[q, pl.ds(i, 1), :] = jnp.full((1, LANES), map_ref[0, q * inner + i], jnp.int32)
     map_copies = []
     for d in range(1, n_ctg):
         copy = to_ctg(map_send.at[other_c(d)], map_recv.at[me_c], map_ssem.at[d], map_rsem.at[d], d)

time: 26.9 us -> 26.9 us (level)
  no operation moved by 1% of the time
where the time goes in v7:
time: 26.9 us; the launch traced here: 26.8 us
  Pallas kernels  26.1 us (97%)
  between operations  0.64 us (2%)
    pallas_call x1, Pallas kernels, per_device_fused(): pl.pallas_call(functools.partial(kernel, n_ctg, n_line, outages, hours),...  23.4 us
    pallas_call x1, Pallas kernels, per_device_fused(): pl.pallas_call(write_out, out_shape=shapes, in_specs=[vmem] * 3, out_spec...  2.76 us

profile of v7, /device:TPU:0, one launch (start us, length us, event | category | flops | bytes accessed | tf_op | source)
XLA Modules:
  0.0 26.8 jit_solution(13119604528339386709)
XLA Ops:
  0.6 23.4 %dual_step.1 = (f32[8,12,128,128]{3,2,1,0:T(8,128)S(1)}, f32[120,128]{1,0:T(8,128)S(1)}, f32[12,128]{1,0:T(8,128)S(1)}) custom-call(s32[1,40]{1,0:T(1,128)} %map_hbm.1, s32[4]{0:T(128)} %owner_hbm.1, s32[1,128]{1,0:T(1,128)} %bitcast.7, f32[40,128]{1,0:T(8,128)} %bitcast.6, f32[120,128]{1,0:T(8,128)} %bitcast.5, bf16[1,8,128,128]{3,2,1,0:T(8,128)(2,1)} %lodf_hbm.1, ...), custom_call_target="tpu_custom_call" | custom-call | tf_op jit(solution)/shard_map/dual_step/pallas_call | solution.py:365
  24.0 2.8 %write_out.1 = (f32[8,12,128,128]{3,2,1,0:T(8,128)}, f32[120,128]{1,0:T(8,128)}, f32[12,128]{1,0:T(8,128)}) custom-call(f32[8,12,128,128]{3,2,1,0:T(8,128)S(1)} %get-tuple-element.9.new_vmem, f32[120,128]{1,0:T(8,128)S(1)} %get-tuple-element.10.line_vmem, f32[12,128]{1,0:T(8,128)S(1)} %get-tuple-element.11.grad_vmem), custom_call_target="tpu_custom_call" | custom-call | tf_op jit(solution)/shard_map/write_out/pallas_call | solution.py:410
